TPU v7x, 32 devices: a whole 2x2x4 slice. The times are simulated.
32 devices in a mesh: groups: 2 (over y), space: 4 (over z), tm: 2 (over x), probe: 2 (over core).
Axes of the slice: x: 2, y: 2, z: 4, core: 2. Of those that a mesh axis runs over, the one named last changes fastest.
Arguments:
- points: float32 [16, 32, 3, 256], P(('groups', 'space'), 'tm'), parts along dimension 0, may hold values from 0 to 512, as said below
- probes: bfloat16 [16, 32, 8, 256], P(('groups', 'space'), 'tm', 'probe'), parts along dimension 0, may hold values from -6 to 6
- basis: bfloat16 [16, 32, 64, 256], P(('groups', 'space'), 'tm'), parts along dimension 0, may hold values from -0.375 to 0.375
- transfer: bfloat16 [16, 32, 64, 64], P(('groups', 'space'), 'tm'), parts along dimension 0, may hold values from -0.5 to 0.5
- coupling0: bfloat16 [16, 32, 12, 64, 64], P(('groups', 'space'), 'tm'), parts along dimension 0, may hold values from -0.21875 to 0.21875
- list0: int32 [16, 32, 12], P(('groups', 'space'), 'tm'), parts along dimension 0, may hold values from -1 to 255, as said below
- coupling1: bfloat16 [8, 2, 6, 64, 64], P(('groups', 'space'), 'tm'), parts along dimension 0, may hold values from -0.3125 to 0.3125
- list1: int32 [8, 2, 6], P(('groups', 'space'), 'tm'), parts along dimension 0, may hold values from -1 to 7, as said below
- near: int32 [16, 32, 9], P(('groups', 'space'), 'tm'), parts along dimension 0, may hold values from 0 to 255, as said below
Outputs:
- product: float32 [16, 32, 8, 256], P(('groups', 'space'), 'tm', 'probe'), parts along dimension 0
There are 2 independent parts, one for each index of `groups`. A program takes and returns all parts, laid end to end along the dimension named above; each array names one. Nothing has to cross between parts.
Inputs may be any that keep to these rules, and one draw needn't show every extreme that they name: `points`: leaf (a, b) has its first coordinate in [a 16, (a + 1) * 16), its second in [0, 32), its third in [b * 16, (b + 1) * 16). `near`: the 9 entries of leaf (a, b) are distinct leaves (a2, b2) with |a2 - a| <= 2 and |b2 - b| <= 2. `list0`: -1 pads. Other entries of leaf (a, b) are distinct leaves (a2, b2) with |a2 - a| <= 5 and |b2 - b| <= 5, and |a2 - a| > 2 or |b2 - b| > 2; each leaf has 6 to 12 of them. `list1`: -1 pads. Other entries are distinct nodes other than the node itself; each node has 3 to 6 of them.
All inputs are finite; a program needn't handle non-finite values.
Results may differ from a plain program's by a relative error of at most 0.0044.
Values may be sent and summed in bfloat16 or wider, within the bound.
A program may use at most 64 MiB of HBM per device.

v0:
```python
import jax
import jax.numpy as jnp
from jax import lax
from jax.sharding import PartitionSpec as P

M0 = 12
M1 = 6
CELL = 16


def padded(value, sides, width):
    for axis, dim in sides:
        count, length = (lax.axis_size(axis), value.shape[dim])
        up = [(i, (i + 1) % count) for i in range(count - 1)]
        down = [(j, i) for i, j in up]
        last = lax.slice_in_dim(value, length - width, length, axis=dim)
        leading = lax.slice_in_dim(value, 0, width, axis=dim)
        before = lax.ppermute(last, axis, up)
        after = lax.ppermute(leading, axis, down)
        value = jnp.concatenate([before, value, after], axis=dim)
    return value


def kernel_block(own, other):
    space_rate = 1.0 / (4.5 * CELL * CELL)
    time_rate = 1.0 / (2.0 * CELL * CELL)
    east = own[..., 0, :, None] - other[..., 0, None, :]
    north = own[..., 1, :, None] - other[..., 1, None, :]
    hours = own[..., 2, :, None] - other[..., 2, None, :]
    value = 0.1 * jnp.exp(-(east * east + north * north) * space_rate - hours * hours * time_rate)
    return value.astype(jnp.bfloat16)


def on_device(points, probes, basis, transfer, coupling0, list0, coupling1, list1, near):
    rows_a, rows_b = (points.shape[0], points.shape[1])
    probe_count, rank, width = (probes.shape[2], basis.shape[2], basis.shape[3])
    count = rows_a * rows_b
    tm_size = lax.axis_size("tm")
    space_at = lax.axis_index("space")
    time_at = lax.axis_index("tm")
    columns = rows_b * tm_size
    coef = jnp.einsum("abrp,abkp->abrk", probes, basis, preferred_element_type=jnp.float32).astype(
        jnp.bfloat16
    )
    coef_rows = coef.reshape(count, probe_count * rank)
    padded_pts = padded(points, (("space", 0), ("tm", 1)), 2)
    padded_prb = padded(probes, (("space", 0), ("tm", 1)), 2)
    flat_pts = padded_pts.reshape(-1, 3, width)
    flat_prb = padded_prb.reshape(-1, probe_count, width)
    row_base = space_at * rows_a - 2
    col_base = time_at * rows_b - 2
    spots = (near // columns - row_base) * (rows_b + 4) + (near % columns - col_base)

    def near_column(carry, step):
        own = lax.dynamic_index_in_dim(points, step, 1, keepdims=False)
        where_from = lax.dynamic_index_in_dim(spots, step, 1, keepdims=False)
        other = flat_pts[where_from]
        vectors = flat_prb[where_from]
        kern = kernel_block(own[:, None], other)
        return (
            carry,
            jnp.einsum("anpq,anrq->arp", kern, vectors, preferred_element_type=jnp.float32),
        )

    _, near_cols = lax.scan(near_column, 0, jnp.arange(rows_b, dtype=jnp.int32))
    near_part = jnp.transpose(near_cols, (1, 0, 2, 3))
    wanted = list0.reshape(count, M0)
    piece = lax.all_gather(coef_rows, ("space", "tm"), axis=0, tiled=True)
    rows = jnp.arange(piece.shape[0], dtype=jnp.int32)
    owner = rows // count
    local = rows % count
    ids = (
        (owner // tm_size * rows_a + local // rows_b) * columns
        + owner % tm_size * rows_b
        + local % rows_b
    )
    hits = (wanted[:, :, None] == ids[None, None, :]).astype(jnp.bfloat16)
    picked = jnp.einsum("lmn,nc->lmc", hits, piece, preferred_element_type=jnp.float32)
    chosen = picked.astype(jnp.bfloat16).reshape(count, M0, probe_count, rank)
    level_zero = jnp.einsum(
        "lmkq,lmrq->lrk",
        coupling0.reshape(count, M0, rank, rank),
        chosen,
        preferred_element_type=jnp.float32,
    )
    steps_up = transfer.reshape(count, rank, rank)
    node_coef = jnp.einsum(
        "lkq,lrq->rk",
        steps_up,
        coef.reshape(count, probe_count, rank),
        preferred_element_type=jnp.float32,
    )
    node_coef = node_coef.astype(jnp.bfloat16).reshape(1, probe_count * rank)
    all_nodes = lax.all_gather(node_coef, ("space", "tm"), axis=0, tiled=True)
    node_ids = jnp.arange(all_nodes.shape[0], dtype=jnp.int32)
    node_hits = (list1.reshape(-1)[:, None] == node_ids[None, :]).astype(jnp.bfloat16)
    chosen_nodes = jnp.dot(node_hits, all_nodes, preferred_element_type=jnp.float32).astype(
        jnp.bfloat16
    )
    chosen_nodes = chosen_nodes.reshape(M1, probe_count, rank)
    level_one = jnp.einsum(
        "mkq,mrq->rk",
        coupling1.reshape(M1, rank, rank),
        chosen_nodes,
        preferred_element_type=jnp.float32,
    ).astype(jnp.bfloat16)
    downward = jnp.einsum("lkq,rk->lrq", steps_up, level_one, preferred_element_type=jnp.float32)
    total = (level_zero + downward).astype(jnp.bfloat16)
    far_part = jnp.einsum(
        "lrk,lkp->lrp", total, basis.reshape(count, rank, width), preferred_element_type=jnp.float32
    )
    return far_part.reshape(rows_a, rows_b, probe_count, width) + near_part


def solution(mesh):
    in_specs = (
        P(("groups", "space"), "tm", None, None),
        P(("groups", "space"), "tm", "probe", None),
        P(("groups", "space"), "tm", None, None),
        P(("groups", "space"), "tm", None, None),
        P(("groups", "space"), "tm", None, None, None),
        P(("groups", "space"), "tm", None),
        P(("groups", "space"), "tm", None, None, None),
        P(("groups", "space"), "tm", None),
        P(("groups", "space"), "tm", None),
    )
    out_specs = P(("groups", "space"), "tm", "probe", None)
    return jax.shard_map(
        on_device, mesh=mesh, in_specs=in_specs, out_specs=out_specs, check_vma=False
    )
```

profile of v0, /device:TPU:0, one launch (start us, length us, event | category | flops | bytes accessed | tf_op | source)
XLA Modules:
  0.0 197.6 jit_solution(5362807903784805871)
XLA Ops:
  0.0 5.1 %collective-permute-start.4 = (f32[2,16,3,256]{3,1,2,0:T(8,128)}, f32[2,16,3,256]{3,1,2,0:T(8,128)S(1)}, u32[]{:S(2)}, u32[]{:S(2)}) collective-permute-start(f32[2,16,3,256]{3,1,2,0:T(8,128)} %param.11), channel_id=1, source_target_pairs={{0,4},{4,8},{8,12},{1,5},{5,9},{9,13},{2,6},{6,10},{10,14},{3,7},{... | collective-permute-start | bytes 294920 | tf_op jit(solution)/shard_map/ppermute | solution.py:18
  5.1 1.3 collective-permute-start.5
  6.4 4.6 %collective-permute-start = (bf16[2,16,4,256]{3,2,1,0:T(4,128)(2,1)}, bf16[2,16,4,256]{3,2,1,0:T(4,128)(2,1)S(1)}, u32[]{:S(2)}, u32[]{:S(2)}) collective-permute-start(bf16[2,16,4,256]{3,2,1,0:T(4,128)(2,1)} %param.12), channel_id=1, source_target_pairs={{0,4},{4,8},{8,12},{1,5},{5,9},{9,13},{2,6},{6,10},{10,14},{3,7},{... | collective-permute-start | bytes 196616 | tf_op jit(solution)/shard_map/ppermute | solution.py:18
  10.9 1.3 collective-permute-start.1
  12.3 0.8 copy.38
  13.1 1.2 convolution_convert_fusion.1
  14.4 32.1 %all_gather.6 = bf16[256,256]{1,0:T(8,128)(2,1)S(1)} all-gather(bf16[32,256]{1,0:T(8,128)(2,1)S(1)} %reshape.145), channel_id=1, replica_groups=mesh['groups'=2,'space'=4,'tm'=2,'probe'=2] {'space','tm'}, dimensions={0}, use_global_device_ids=true | all-gather | bytes 147456 | tf_op jit(solution)/shard_map/all_gather | solution.py:68
  46.5 0.8 eq.36
  47.8 1.3 fusion.16
  49.1 20.4 %all-gather = bf16[8,1,256]{2,1,0:T(2,128)(2,1)S(1)} all-gather(bf16[1,1,256]{2,1,0:T(2,128)(2,1)S(1)} %reshape.174), channel_id=1, replica_groups=mesh['groups'=2,'space'=4,'tm'=2,'probe'=2] {'space','tm'}, dimensions={0}, use_global_device_ids=true | all-gather | bytes 4608 | tf_op jit(solution)/shard_map/all_gather | solution.py:94
  69.5 0.8 convolution_convert_fusion.2
  70.5 4.5 %fusion.9 = f32[32,4,64]{2,1,0:T(4,128)S(1)} fusion(bf16[32,12,4,64]{3,2,0,1:T(4,128)(2,1)S(1)} %reshape.146, bf16[32,12,64,64]{3,2,1,0:T(8,128)(2,1)} %bitcast.116), kind=kOutput, calls=%fused_computation.25 | convolution fusion | flops 12582912 | bytes 3375104 | tf_op jit(solution)/shard_map/lmkq,lmrq->lrk/dot_general | solution.py:80
  75.8 1.3 collective-permute-start.2
  77.1 1.3 collective-permute-start.3
  78.5 4.5 %collective-permute-start.6 = (f32[6,2,3,256]{3,1,2,0:T(2,128)S(1)}, f32[6,2,3,256]{3,1,2,0:T(2,128)S(1)}, u32[]{:S(2)}, u32[]{:S(2)}) collective-permute-start(f32[6,2,3,256]{3,1,2,0:T(2,128)S(1)} %get-tuple-element.88), channel_id=1, source_target_pairs={{0,2},{1,3},{4,6},{5,7},{8,10},{9,11},{12,14},{13,15},{16,18},{17,... | collective-permute-start | bytes 110600 | tf_op jit(solution)/shard_map/ppermute | solution.py:18
  83.1 1.3 collective-permute-start.7
  84.7 4.2 %collective-permute-done.7 = f32[6,2,3,256]{3,1,2,0:T(2,128)S(1)} collective-permute-done((f32[6,2,3,256]{3,1,2,0:T(2,128)S(1)}, f32[6,2,3,256]{3,1,2,0:T(2,128)S(1)}, u32[]{:S(2)}, u32[]{:S(2)}) %collective-permute-start.7) | collective-permute-done | bytes 36896 | tf_op jit(solution)/shard_map/ppermute | solution.py:19
  89.2 107.7 %while.10 = (s32[]{:T(128)}, f32[16,2,4,256]{3,2,0,1:T(4,128)S(1)}, s32[16]{0:T(128)S(1)}, s32[2,16,9]{2,0,1:T(2,128)S(1)}, bf16[120,4,256]{2,1,0:T(4,128)(2,1)S...) while((s32[]{:T(128)}, f32[16,2,4,256]{3,2,0,1:T(4,128)S(1)}, ...), condition=%wide.region_1.2_spmd, body=%wide.region_0.1_spmd.sunk | while | flops 24773692 | bytes 694983 | solution.py:65
  89.2 0.7 dynamic_slice.20
  92.8 0.6 gather_fusion
  93.4 2.5 %fusion.52 = f32[16,2,4,256]{3,2,0,1:T(4,128)S(1)} fusion(f32[16,2,4,256]{3,2,0,1:T(4,128)S(1)} %get-tuple-element.168, s32[]{:T(128)} %get-tuple-element.167, bf16[2,9,4,256]{3,2,1,0:T(4,128)(2,1)S(1)} %bitcast.111, f32[2,9,256]{2,1,0:T(8,128)S(1)} %copy.82, f32[2,256]{1,0:T(2,128)S(1)} %get-tuple-element.150, f32[2,9,256]{2,1,0:T(8,128)S(1)} %copy.83, ...), kind=kOutput, calls=%fused_computation.5.clone.1 | convolution fusion | flops 24772608 | bytes 149508 | tf_op jit(solution)/shard_map/while/body/eval_jaxpr/anpq,anrq->arp/dot_general | solution.py:62
  95.9 0.7 dynamic_slice.20
  99.6 0.6 gather_fusion
  100.2 2.5 %fusion.52 = f32[16,2,4,256]{3,2,0,1:T(4,128)S(1)} fusion(f32[16,2,4,256]{3,2,0,1:T(4,128)S(1)} %get-tuple-element.168, s32[]{:T(128)} %get-tuple-element.167, bf16[2,9,4,256]{3,2,1,0:T(4,128)(2,1)S(1)} %bitcast.111, f32[2,9,256]{2,1,0:T(8,128)S(1)} %copy.82, f32[2,256]{1,0:T(2,128)S(1)} %get-tuple-element.150, f32[2,9,256]{2,1,0:T(8,128)S(1)} %copy.83, ...), kind=kOutput, calls=%fused_computation.5.clone.1 | convolution fusion | flops 24772608 | bytes 149508 | tf_op jit(solution)/shard_map/while/body/eval_jaxpr/anpq,anrq->arp/dot_general | solution.py:62
  102.7 0.7 dynamic_slice.20
  106.3 0.6 gather_fusion
  106.9 2.5 %fusion.52 = f32[16,2,4,256]{3,2,0,1:T(4,128)S(1)} fusion(f32[16,2,4,256]{3,2,0,1:T(4,128)S(1)} %get-tuple-element.168, s32[]{:T(128)} %get-tuple-element.167, bf16[2,9,4,256]{3,2,1,0:T(4,128)(2,1)S(1)} %bitcast.111, f32[2,9,256]{2,1,0:T(8,128)S(1)} %copy.82, f32[2,256]{1,0:T(2,128)S(1)} %get-tuple-element.150, f32[2,9,256]{2,1,0:T(8,128)S(1)} %copy.83, ...), kind=kOutput, calls=%fused_computation.5.clone.1 | convolution fusion | flops 24772608 | bytes 149508 | tf_op jit(solution)/shard_map/while/body/eval_jaxpr/anpq,anrq->arp/dot_general | solution.py:62
  109.4 0.7 dynamic_slice.20
  113.0 0.6 gather_fusion
  113.6 2.5 %fusion.52 = f32[16,2,4,256]{3,2,0,1:T(4,128)S(1)} fusion(f32[16,2,4,256]{3,2,0,1:T(4,128)S(1)} %get-tuple-element.168, s32[]{:T(128)} %get-tuple-element.167, bf16[2,9,4,256]{3,2,1,0:T(4,128)(2,1)S(1)} %bitcast.111, f32[2,9,256]{2,1,0:T(8,128)S(1)} %copy.82, f32[2,256]{1,0:T(2,128)S(1)} %get-tuple-element.150, f32[2,9,256]{2,1,0:T(8,128)S(1)} %copy.83, ...), kind=kOutput, calls=%fused_computation.5.clone.1 | convolution fusion | flops 24772608 | bytes 149508 | tf_op jit(solution)/shard_map/while/body/eval_jaxpr/anpq,anrq->arp/dot_general | solution.py:62
  116.1 0.7 dynamic_slice.20
  119.8 0.6 gather_fusion
  120.4 2.5 %fusion.52 = f32[16,2,4,256]{3,2,0,1:T(4,128)S(1)} fusion(f32[16,2,4,256]{3,2,0,1:T(4,128)S(1)} %get-tuple-element.168, s32[]{:T(128)} %get-tuple-element.167, bf16[2,9,4,256]{3,2,1,0:T(4,128)(2,1)S(1)} %bitcast.111, f32[2,9,256]{2,1,0:T(8,128)S(1)} %copy.82, f32[2,256]{1,0:T(2,128)S(1)} %get-tuple-element.150, f32[2,9,256]{2,1,0:T(8,128)S(1)} %copy.83, ...), kind=kOutput, calls=%fused_computation.5.clone.1 | convolution fusion | flops 24772608 | bytes 149508 | tf_op jit(solution)/shard_map/while/body/eval_jaxpr/anpq,anrq->arp/dot_general | solution.py:62
  122.9 0.7 dynamic_slice.20
  126.5 0.6 gather_fusion
  127.1 2.5 %fusion.52 = f32[16,2,4,256]{3,2,0,1:T(4,128)S(1)} fusion(f32[16,2,4,256]{3,2,0,1:T(4,128)S(1)} %get-tuple-element.168, s32[]{:T(128)} %get-tuple-element.167, bf16[2,9,4,256]{3,2,1,0:T(4,128)(2,1)S(1)} %bitcast.111, f32[2,9,256]{2,1,0:T(8,128)S(1)} %copy.82, f32[2,256]{1,0:T(2,128)S(1)} %get-tuple-element.150, f32[2,9,256]{2,1,0:T(8,128)S(1)} %copy.83, ...), kind=kOutput, calls=%fused_computation.5.clone.1 | convolution fusion | flops 24772608 | bytes 149508 | tf_op jit(solution)/shard_map/while/body/eval_jaxpr/anpq,anrq->arp/dot_general | solution.py:62
  129.6 0.7 dynamic_slice.20
  132.4 0.6 gather_fusion.1
  133.2 0.6 gather_fusion
  133.8 2.5 %fusion.52 = f32[16,2,4,256]{3,2,0,1:T(4,128)S(1)} fusion(f32[16,2,4,256]{3,2,0,1:T(4,128)S(1)} %get-tuple-element.168, s32[]{:T(128)} %get-tuple-element.167, bf16[2,9,4,256]{3,2,1,0:T(4,128)(2,1)S(1)} %bitcast.111, f32[2,9,256]{2,1,0:T(8,128)S(1)} %copy.82, f32[2,256]{1,0:T(2,128)S(1)} %get-tuple-element.150, f32[2,9,256]{2,1,0:T(8,128)S(1)} %copy.83, ...), kind=kOutput, calls=%fused_computation.5.clone.1 | convolution fusion | flops 24772608 | bytes 149508 | tf_op jit(solution)/shard_map/while/body/eval_jaxpr/anpq,anrq->arp/dot_general | solution.py:62
  136.3 0.7 dynamic_slice.20
  139.9 0.6 gather_fusion
  140.6 2.5 %fusion.52 = f32[16,2,4,256]{3,2,0,1:T(4,128)S(1)} fusion(f32[16,2,4,256]{3,2,0,1:T(4,128)S(1)} %get-tuple-element.168, s32[]{:T(128)} %get-tuple-element.167, bf16[2,9,4,256]{3,2,1,0:T(4,128)(2,1)S(1)} %bitcast.111, f32[2,9,256]{2,1,0:T(8,128)S(1)} %copy.82, f32[2,256]{1,0:T(2,128)S(1)} %get-tuple-element.150, f32[2,9,256]{2,1,0:T(8,128)S(1)} %copy.83, ...), kind=kOutput, calls=%fused_computation.5.clone.1 | convolution fusion | flops 24772608 | bytes 149508 | tf_op jit(solution)/shard_map/while/body/eval_jaxpr/anpq,anrq->arp/dot_general | solution.py:62
  143.0 0.7 dynamic_slice.20
  146.7 0.6 gather_fusion
  147.3 2.5 %fusion.52 = f32[16,2,4,256]{3,2,0,1:T(4,128)S(1)} fusion(f32[16,2,4,256]{3,2,0,1:T(4,128)S(1)} %get-tuple-element.168, s32[]{:T(128)} %get-tuple-element.167, bf16[2,9,4,256]{3,2,1,0:T(4,128)(2,1)S(1)} %bitcast.111, f32[2,9,256]{2,1,0:T(8,128)S(1)} %copy.82, f32[2,256]{1,0:T(2,128)S(1)} %get-tuple-element.150, f32[2,9,256]{2,1,0:T(8,128)S(1)} %copy.83, ...), kind=kOutput, calls=%fused_computation.5.clone.1 | convolution fusion | flops 24772608 | bytes 149508 | tf_op jit(solution)/shard_map/while/body/eval_jaxpr/anpq,anrq->arp/dot_general | solution.py:62
  149.8 0.7 dynamic_slice.20
  154.0 2.5 %fusion.52 = f32[16,2,4,256]{3,2,0,1:T(4,128)S(1)} fusion(f32[16,2,4,256]{3,2,0,1:T(4,128)S(1)} %get-tuple-element.168, s32[]{:T(128)} %get-tuple-element.167, bf16[2,9,4,256]{3,2,1,0:T(4,128)(2,1)S(1)} %bitcast.111, f32[2,9,256]{2,1,0:T(8,128)S(1)} %copy.82, f32[2,256]{1,0:T(2,128)S(1)} %get-tuple-element.150, f32[2,9,256]{2,1,0:T(8,128)S(1)} %copy.83, ...), kind=kOutput, calls=%fused_computation.5.clone.1 | convolution fusion | flops 24772608 | bytes 149508 | tf_op jit(solution)/shard_map/while/body/eval_jaxpr/anpq,anrq->arp/dot_general | solution.py:62
  156.5 0.7 dynamic_slice.20
  160.7 2.5 %fusion.52 = f32[16,2,4,256]{3,2,0,1:T(4,128)S(1)} fusion(f32[16,2,4,256]{3,2,0,1:T(4,128)S(1)} %get-tuple-element.168, s32[]{:T(128)} %get-tuple-element.167, bf16[2,9,4,256]{3,2,1,0:T(4,128)(2,1)S(1)} %bitcast.111, f32[2,9,256]{2,1,0:T(8,128)S(1)} %copy.82, f32[2,256]{1,0:T(2,128)S(1)} %get-tuple-element.150, f32[2,9,256]{2,1,0:T(8,128)S(1)} %copy.83, ...), kind=kOutput, calls=%fused_computation.5.clone.1 | convolution fusion | flops 24772608 | bytes 149508 | tf_op jit(solution)/shard_map/while/body/eval_jaxpr/anpq,anrq->arp/dot_general | solution.py:62
  163.2 0.7 dynamic_slice.20
  166.9 0.6 gather_fusion
  167.5 2.5 %fusion.52 = f32[16,2,4,256]{3,2,0,1:T(4,128)S(1)} fusion(f32[16,2,4,256]{3,2,0,1:T(4,128)S(1)} %get-tuple-element.168, s32[]{:T(128)} %get-tuple-element.167, bf16[2,9,4,256]{3,2,1,0:T(4,128)(2,1)S(1)} %bitcast.111, f32[2,9,256]{2,1,0:T(8,128)S(1)} %copy.82, f32[2,256]{1,0:T(2,128)S(1)} %get-tuple-element.150, f32[2,9,256]{2,1,0:T(8,128)S(1)} %copy.83, ...), kind=kOutput, calls=%fused_computation.5.clone.1 | convolution fusion | flops 24772608 | bytes 149508 | tf_op jit(solution)/shard_map/while/body/eval_jaxpr/anpq,anrq->arp/dot_general | solution.py:62
  170.0 0.7 dynamic_slice.20
  174.2 2.5 %fusion.52 = f32[16,2,4,256]{3,2,0,1:T(4,128)S(1)} fusion(f32[16,2,4,256]{3,2,0,1:T(4,128)S(1)} %get-tuple-element.168, s32[]{:T(128)} %get-tuple-element.167, bf16[2,9,4,256]{3,2,1,0:T(4,128)(2,1)S(1)} %bitcast.111, f32[2,9,256]{2,1,0:T(8,128)S(1)} %copy.82, f32[2,256]{1,0:T(2,128)S(1)} %get-tuple-element.150, f32[2,9,256]{2,1,0:T(8,128)S(1)} %copy.83, ...), kind=kOutput, calls=%fused_computation.5.clone.1 | convolution fusion | flops 24772608 | bytes 149508 | tf_op jit(solution)/shard_map/while/body/eval_jaxpr/anpq,anrq->arp/dot_general | solution.py:62
  176.7 0.7 dynamic_slice.20
  180.3 0.6 gather_fusion
  180.9 2.5 %fusion.52 = f32[16,2,4,256]{3,2,0,1:T(4,128)S(1)} fusion(f32[16,2,4,256]{3,2,0,1:T(4,128)S(1)} %get-tuple-element.168, s32[]{:T(128)} %get-tuple-element.167, bf16[2,9,4,256]{3,2,1,0:T(4,128)(2,1)S(1)} %bitcast.111, f32[2,9,256]{2,1,0:T(8,128)S(1)} %copy.82, f32[2,256]{1,0:T(2,128)S(1)} %get-tuple-element.150, f32[2,9,256]{2,1,0:T(8,128)S(1)} %copy.83, ...), kind=kOutput, calls=%fused_computation.5.clone.1 | convolution fusion | flops 24772608 | bytes 149508 | tf_op jit(solution)/shard_map/while/body/eval_jaxpr/anpq,anrq->arp/dot_general | solution.py:62
  183.4 0.7 dynamic_slice.20
  187.0 0.6 gather_fusion
  187.7 2.5 %fusion.52 = f32[16,2,4,256]{3,2,0,1:T(4,128)S(1)} fusion(f32[16,2,4,256]{3,2,0,1:T(4,128)S(1)} %get-tuple-element.168, s32[]{:T(128)} %get-tuple-element.167, bf16[2,9,4,256]{3,2,1,0:T(4,128)(2,1)S(1)} %bitcast.111, f32[2,9,256]{2,1,0:T(8,128)S(1)} %copy.82, f32[2,256]{1,0:T(2,128)S(1)} %get-tuple-element.150, f32[2,9,256]{2,1,0:T(8,128)S(1)} %copy.83, ...), kind=kOutput, calls=%fused_computation.5.clone.1 | convolution fusion | flops 24772608 | bytes 149508 | tf_op jit(solution)/shard_map/while/body/eval_jaxpr/anpq,anrq->arp/dot_general | solution.py:62
  190.2 0.7 dynamic_slice.20
  194.4 2.5 %fusion.52 = f32[16,2,4,256]{3,2,0,1:T(4,128)S(1)} fusion(f32[16,2,4,256]{3,2,0,1:T(4,128)S(1)} %get-tuple-element.168, s32[]{:T(128)} %get-tuple-element.167, bf16[2,9,4,256]{3,2,1,0:T(4,128)(2,1)S(1)} %bitcast.111, f32[2,9,256]{2,1,0:T(8,128)S(1)} %copy.82, f32[2,256]{1,0:T(2,128)S(1)} %get-tuple-element.150, f32[2,9,256]{2,1,0:T(8,128)S(1)} %copy.83, ...), kind=kOutput, calls=%fused_computation.5.clone.1 | convolution fusion | flops 24772608 | bytes 149508 | tf_op jit(solution)/shard_map/while/body/eval_jaxpr/anpq,anrq->arp/dot_general | solution.py:62
  196.9 0.7 bitcast_add_fusion
  (250 shorter events, 16.8 us)
Async XLA Ops:
  0.0 13.0 %copy-start = (bf16[2,16,64,256]{3,2,1,0:T(8,128)(2,1)S(1)}, bf16[2,16,64,256]{3,2,1,0:T(8,128)(2,1)}, u32[]{:S(2)}) copy-start(bf16[2,16,64,256]{3,2,1,0:T(8,128)(2,1)} %param.13) | copy-start | bytes 3145732
  0.0 78.4 %collective-permute-start.4 = (f32[2,16,3,256]{3,1,2,0:T(8,128)}, f32[2,16,3,256]{3,1,2,0:T(8,128)S(1)}, u32[]{:S(2)}, u32[]{:S(2)}) collective-permute-start(f32[2,16,3,256]{3,1,2,0:T(8,128)} %param.11), channel_id=1, source_target_pairs={{0,4},{4,8},{8,12},{1,5},{5,9},{9,13},{2,6},{6,10},{10,14},{3,7},{... | collective-permute-start | bytes 294920 | tf_op jit(solution)/shard_map/ppermute | solution.py:18
  5.1 73.4 %collective-permute-start.5 = (f32[2,16,3,256]{3,1,2,0:T(8,128)}, f32[2,16,3,256]{3,1,2,0:T(8,128)S(1)}, u32[]{:S(2)}, u32[]{:S(2)}) collective-permute-start(f32[2,16,3,256]{3,1,2,0:T(8,128)} %param.11), channel_id=1, source_target_pairs={{4,0},{8,4},{12,8},{5,1},{9,5},{13,9},{6,2},{10,6},{14,10},{7,3},{... | collective-permute-start | bytes 294920 | tf_op jit(solution)/shard_map/ppermute | solution.py:19
  6.4 69.3 %collective-permute-start = (bf16[2,16,4,256]{3,2,1,0:T(4,128)(2,1)}, bf16[2,16,4,256]{3,2,1,0:T(4,128)(2,1)S(1)}, u32[]{:S(2)}, u32[]{:S(2)}) collective-permute-start(bf16[2,16,4,256]{3,2,1,0:T(4,128)(2,1)} %param.12), channel_id=1, source_target_pairs={{0,4},{4,8},{8,12},{1,5},{5,9},{9,13},{2,6},{6,10},{10,14},{3,7},{... | collective-permute-start | bytes 196616 | tf_op jit(solution)/shard_map/ppermute | solution.py:18
  10.9 64.8 %collective-permute-start.1 = (bf16[2,16,4,256]{3,2,1,0:T(4,128)(2,1)}, bf16[2,16,4,256]{3,2,1,0:T(4,128)(2,1)S(1)}, u32[]{:S(2)}, u32[]{:S(2)}) collective-permute-start(bf16[2,16,4,256]{3,2,1,0:T(4,128)(2,1)} %param.12), channel_id=1, source_target_pairs={{4,0},{8,4},{12,8},{5,1},{9,5},{13,9},{6,2},{10,6},{14,10},{7,3},{... | collective-permute-start | bytes 196616 | tf_op jit(solution)/shard_map/ppermute | solution.py:19
  13.0 61.9 %copy-start.4 = (bf16[1,1,6,64,64]{4,3,2,1,0:T(8,128)(2,1)S(1)}, bf16[1,1,6,64,64]{4,3,2,1,0:T(8,128)(2,1)}, u32[]{:S(2)}) copy-start(bf16[1,1,6,64,64]{4,3,2,1,0:T(8,128)(2,1)} %param.17) | copy-start | bytes 147460
  14.3 60.8 %copy-start.1 = (bf16[2,16,64,64]{3,2,1,0:T(8,128)(2,1)S(1)}, bf16[2,16,64,64]{3,2,1,0:T(8,128)(2,1)}, u32[]{:S(2)}) copy-start(bf16[2,16,64,64]{3,2,1,0:T(8,128)(2,1)} %param.14) | copy-start | bytes 786436
  49.1 26.6 %copy-start.2 = (bf16[2,16,4,256]{3,2,1,0:T(4,128)(2,1)S(1)}, bf16[2,16,4,256]{3,2,1,0:T(4,128)(2,1)}, u32[]{:S(2)}) copy-start(bf16[2,16,4,256]{3,2,1,0:T(4,128)(2,1)} %param.12) | copy-start | bytes 196612
  70.5 8.0 %copy-start.3 = (f32[2,16,3,256]{3,1,2,0:T(8,128)S(1)}, f32[2,16,3,256]{3,1,2,0:T(8,128)}, u32[]{:S(2)}) copy-start(f32[2,16,3,256]{3,1,2,0:T(8,128)} %param.11) | copy-start | bytes 294916
  75.8 8.6 %collective-permute-start.2 = (bf16[6,2,4,256]{3,2,1,0:T(4,128)(2,1)S(1)}, bf16[6,2,4,256]{3,2,1,0:T(4,128)(2,1)S(1)}, u32[]{:S(2)}, u32[]{:S(2)}) collective-permute-start(bf16[6,2,4,256]{3,2,1,0:T(4,128)(2,1)S(1)} %get-tuple-element.90), channel_id=1, source_target_pairs={{0,2},{1,3},{4,6},{5,7},{8,10},{9,11},{12,14},{13,15},{16,18},{17,... | collective-permute-start | bytes 73736 | tf_op jit(solution)/shard_map/ppermute | solution.py:18
  77.1 7.3 %collective-permute-start.3 = (bf16[6,2,4,256]{3,2,1,0:T(4,128)(2,1)S(1)}, bf16[6,2,4,256]{3,2,1,0:T(4,128)(2,1)S(1)}, u32[]{:S(2)}, u32[]{:S(2)}) collective-permute-start(bf16[6,2,4,256]{3,2,1,0:T(4,128)(2,1)S(1)} %get-tuple-element.91), channel_id=1, source_target_pairs={{2,0},{3,1},{6,4},{7,5},{10,8},{11,9},{14,12},{15,13},{18,16},{19,... | collective-permute-start | bytes 73736 | tf_op jit(solution)/shard_map/ppermute | solution.py:19
  78.5 6.2 %collective-permute-start.6 = (f32[6,2,3,256]{3,1,2,0:T(2,128)S(1)}, f32[6,2,3,256]{3,1,2,0:T(2,128)S(1)}, u32[]{:S(2)}, u32[]{:S(2)}) collective-permute-start(f32[6,2,3,256]{3,1,2,0:T(2,128)S(1)} %get-tuple-element.88), channel_id=1, source_target_pairs={{0,2},{1,3},{4,6},{5,7},{8,10},{9,11},{12,14},{13,15},{16,18},{17,... | collective-permute-start | bytes 110600 | tf_op jit(solution)/shard_map/ppermute | solution.py:18
  83.1 5.9 %collective-permute-start.7 = (f32[6,2,3,256]{3,1,2,0:T(2,128)S(1)}, f32[6,2,3,256]{3,1,2,0:T(2,128)S(1)}, u32[]{:S(2)}, u32[]{:S(2)}) collective-permute-start(f32[6,2,3,256]{3,1,2,0:T(2,128)S(1)} %get-tuple-element.89), channel_id=1, source_target_pairs={{2,0},{3,1},{6,4},{7,5},{10,8},{11,9},{14,12},{15,13},{18,16},{19,... | collective-permute-start | bytes 110600 | tf_op jit(solution)/shard_map/ppermute | solution.py:19
where the time goes:
time: 199 us; the launch traced here: 198 us
  blocking collectives  52.5 us (26%)
  matrix products  48.6 us (24%)
  local copies, waits for them, and re-layouts  35.3 us (18%)
  loops' own time  34.6 us (17%)
  starting transfers between devices  20.6 us (10%)
  waiting for transfers between devices  4.36 us (2%)
    dot_general x16, matrix products, near_column(): jnp.einsum('anpq,anrq->arp', kern, vectors, preferred_element_type=jnp.fl...  39.9 us
    another operation x1, loops' own time, on_device(): _, near_cols = lax.scan(near_column, 0, jnp.arange(rows_b, dtype=jnp.int32))  34.6 us
    all_gather x1, blocking collectives, on_device(): piece = lax.all_gather(coef_rows, ('space', 'tm'), axis=0, tiled=True)  32.1 us
    all_gather x1, blocking collectives, on_device(): all_nodes = lax.all_gather(node_coef, ('space', 'tm'), axis=0, tiled=True)  20.4 us
    ppermute x4, starting transfers between devices, padded(): before = lax.ppermute(last, axis, up)  15.4 us
    dynamic_slice x16, local copies, waits for them, and re-layouts, on_device(): _, near_cols = lax.scan(near_column, 0, jnp.arange(rows_b, dtype=jnp.int32))  10.7 us
    gather x16, local copies, waits for them, and re-layouts, near_column(): vectors = flat_prb[where_from]  9.53 us
    gather x16, local copies, waits for them, and re-layouts, near_column(): other = flat_pts[where_from]  9.51 us
  transfers between devices with their start and end apart: 8, of which 2 were waited for; matrix products, arithmetic and copies ran while one was open for 6% of the time, Pallas kernels for 0%

commit v1 on v0

v1 whole, which is shorter than its diff:
```python
import functools
import math

import jax
import jax.numpy as jnp
from jax import lax
from jax.experimental import pallas as pl
from jax.experimental.pallas import tpu as pltpu
from jax.sharding import PartitionSpec as P

CELL = 16
F32 = jnp.float32
BF16 = jnp.bfloat16
MESH = pl.DeviceIdType.MESH
LOG2E = math.log2(math.e)
SPACE_SCALE = math.sqrt(LOG2E / (4.5 * CELL * CELL))
TIME_SCALE = math.sqrt(LOG2E / (2.0 * CELL * CELL))
NODE_ROWS = 48

NT = (((1,), (1,)), ((), ()))


def dot(a, b, dims=(((1,), (0,)), ((), ()))):
    return lax.dot_general(a, b, dims, preferred_element_type=F32)


def split3(x):
    high = x.astype(BF16).astype(F32)
    rest = x - high
    mid = rest.astype(BF16).astype(F32)
    return high, mid, rest - mid


def kernel(
    n_space,
    n_tm,
    slots_ref,
    pack_ref,
    probes_ref,
    basis_ref,
    transfer_ref,
    coupling1_ref,
    rows_ref,
    coupling0_hbm,
    out_ref,
    win,
    other_feat,
    own_feat,
    vectors,
    near_mine,
    near_theirs,
    coef_f32,
    coef_send,
    piece,
    gathered,
    coupling0,
    halo_send,
    halo_recv,
    coef_ssem,
    coef_rsem,
    near_ssem,
    near_rsem,
    local_sem,
):
    space = lax.axis_index("space")
    tm = lax.axis_index("tm")
    core = lax.axis_index("probe")
    node = space * n_tm + tm
    nodes = n_space * n_tm
    leaves_a, leaves_b = basis_ref.shape[0], basis_ref.shape[1]
    count = leaves_a * leaves_b
    half = leaves_b // 2
    pairs = leaves_b // 2
    span = pairs // 2 + 1
    win_pairs = pairs // 2 + 2
    m0 = coupling0_hbm.shape[2]
    m1 = coupling1_ref.shape[2]
    rank = basis_ref.shape[2]

    load0 = pltpu.make_async_copy(coupling0_hbm, coupling0, local_sem.at[0])
    load0.start()

    barrier = pltpu.get_barrier_semaphore()

    def greet(k, carry):
        @pl.when(k != node * 2 + core)
        def _():
            pl.semaphore_signal(
                barrier,
                inc=1,
                device_id={
                    "space": k // (2 * n_tm),
                    "tm": (k // 2) % n_tm,
                    "probe": k % 2,
                },
                device_id_type=MESH,
            )

        return carry

    lax.fori_loop(0, 2 * nodes, greet, 0)
    pl.semaphore_wait(barrier, 2 * nodes - 1)

    def halo_pieces():
        for ds in (-1, 0, 1):
            for dt in (0, -1, 1):
                for to in (0, 1):
                    if dt == 1 and to == 1 or dt == -1 and to == 0:
                        continue
                    yield ds, dt, to

    def exists(ds, dt):
        s, t = space + ds, tm + dt
        return (s >= 0) & (s < n_space) & (t >= 0) & (t < n_tm)

    def halo_copy(ds, dt, to, source, s, t, c):
        if dt == 0:
            first, slot, length = 3 * to, 1 - to, span
        elif dt == 1:
            first, slot, length = pairs - 1, 0, 1
        else:
            first, slot, length = 0, win_pairs - 1, 1
        if dt == 0:
            first = (pairs // 2 - 1) * to
        return pltpu.make_async_remote_copy(
            src_ref=pack_ref.at[:, pl.ds(first, length)],
            dst_ref=win.at[source, pl.ds(2 - 2 * ds, 2), pl.ds(slot, length)],
            send_sem=halo_send.at[ds + 1, dt + 1, to],
            recv_sem=halo_recv.at[source, ds + 1, dt + 1],
            device_id={"space": s, "tm": t, "probe": c},
            device_id_type=MESH,
        )

    own_first = (pairs // 2 - 1) * core
    own_copy = pltpu.make_async_copy(
        pack_ref.at[:, pl.ds(own_first, span)],
        win.at[core, pl.ds(2, 2), pl.ds(1 - core, span)],
        local_sem.at[1],
    )
    own_copy.start()
    for ds, dt, to in halo_pieces():
        ok = exists(ds, dt)
        if ds == 0 and dt == 0:
            ok = core != to

        @pl.when(ok)
        def _(ds=ds, dt=dt, to=to):
            halo_copy(ds, dt, to, core, space + ds, tm + dt, to).start()

    node_sum = jnp.zeros((4, rank), F32)
    for i in range(count):
        a, b = i // leaves_b, i % leaves_b
        value = dot(probes_ref[a, b], basis_ref[a, b], NT).astype(BF16)
        node_sum = node_sum + dot(value, transfer_ref[a, b], NT)
        value = value.astype(F32)
        for r in range(4):
            coef_f32[r // 2, i, pl.ds((r % 2) * rank, rank)] = value[r]
    node_sum = node_sum.astype(BF16).astype(F32)
    for r in range(4):
        coef_f32[r // 2, count, pl.ds((r % 2) * rank, rank)] = node_sum[r]
    coef_f32[:, pl.ds(count + 1, NODE_ROWS - count - 1)] = jnp.zeros(
        (2, NODE_ROWS - count - 1, 2 * rank), F32
    )
    coef_send[...] = coef_f32[...].astype(BF16)

    def coef_copy(at, sem_at, to):
        return pltpu.make_async_remote_copy(
            src_ref=coef_send,
            dst_ref=piece.at[:, pl.ds(pl.multiple_of(at * NODE_ROWS, 16), NODE_ROWS)],
            send_sem=coef_ssem.at[sem_at],
            recv_sem=coef_rsem.at[at],
            device_id={"space": to // n_tm, "tm": to % n_tm, "probe": core},
            device_id_type=MESH,
        )

    def send_coef(k, carry):
        @pl.when(k != node)
        def _():
            coef_copy(node, k, k).start()

        return carry

    lax.fori_loop(0, nodes, send_coef, 0)
    own_coef = pltpu.make_async_copy(
        coef_send,
        piece.at[:, pl.ds(pl.multiple_of(node * NODE_ROWS, 16), NODE_ROWS)],
        local_sem.at[2],
    )
    own_coef.start()

    own_copy.wait()
    for source in (0, 1):
        for ds in (-1, 0, 1):
            for dt in (0, -1, 1):
                ok = exists(-ds, -dt)
                if dt == 1:
                    ok = ok & (core == 0)
                if dt == -1:
                    ok = ok & (core == 1)
                if ds == 0 and dt == 0:
                    ok = core != source

                if dt == 0:
                    for to in (0, 1):

                        @pl.when(ok & (core == to))
                        def _(ds=ds, dt=dt, to=to, source=source):
                            halo_copy(ds, dt, to, source, space, tm, core).wait_recv()
                else:

                    @pl.when(ok)
                    def _(ds=ds, dt=dt, source=source):
                        to = 0 if dt == 1 else 1
                        halo_copy(ds, dt, to, source, space, tm, core).wait_recv()

    row4 = lax.broadcasted_iota(jnp.int32, (4, 1), 0)
    scale = jnp.where(row4 == 2, TIME_SCALE, jnp.where(row4 == 3, 0.0, SPACE_SCALE))
    ones = jnp.where(lax.broadcasted_iota(jnp.int32, (4, 256), 0) < 3, 1.0, 0.0).astype(F32)
    zero1 = jnp.zeros((1, 256), F32)
    mid_a = (leaves_a + 4) / 2.0 - 0.5
    mid_b = (half + 4) / 2.0 - 0.5

    def features(w, j, carry):
        tiles = [win[s, w, j].astype(F32) for s in (0, 1)]
        for e in (0, 1):
            slot = (w * win_pairs + j) * 2 + e
            col = (j * 2 + e).astype(F32)
            place = jnp.where(
                row4 == 0,
                (w - mid_a) * CELL,
                jnp.where(row4 == 2, (col - mid_b) * CELL, 0.0),
            )
            at = (tiles[e][8:12] + tiles[e][12:16] + place) * scale
            high, mid, low = split3(at)
            norm = -jnp.sum(at * at, axis=0, keepdims=True)
            norms = jnp.concatenate([*split3(norm), zero1], axis=0)
            feat = jnp.concatenate([high, mid, low, high, mid, high, norms, ones], axis=0)
            other_feat[slot] = feat.astype(BF16)
            probe_rows = jnp.concatenate(
                [tiles[0][4 * e : 4 * e + 4], tiles[1][4 * e : 4 * e + 4]], axis=0
            )
            vectors[slot] = probe_rows.astype(BF16)
            if 2 <= w < 2 + leaves_a:
                norms = jnp.concatenate([*split3(norm + math.log2(0.1)), zero1], axis=0)
                high, mid, low = 2.0 * high, 2.0 * mid, 2.0 * low
                feat = jnp.concatenate([high, high, high, mid, mid, low, ones, norms], axis=0)
                own_feat[(w - 2) * win_pairs * 2 + j * 2 + e] = feat.T.astype(BF16)
        return carry

    for w in range(leaves_a + 4):
        lax.fori_loop(0, win_pairs, functools.partial(features, w), 0)

    picks = slots_ref.shape[0] // (leaves_a * half)

    def near_leaf(i, carry):
        own = own_feat[i // half * (2 * win_pairs) + i % half + 2]
        total = jnp.zeros((own.shape[0], 8), F32)
        for n in range(picks):
            slot = slots_ref[i * picks + n]
            kern = jnp.exp2(dot(own, other_feat[slot])).astype(BF16)
            total = total + dot(kern, vectors[slot], NT)
        near_mine[i] = total.T
        return carry

    lax.fori_loop(0, leaves_a * half, near_leaf, 0)

    near_copy = pltpu.make_async_remote_copy(
        src_ref=near_mine,
        dst_ref=near_theirs,
        send_sem=near_ssem,
        recv_sem=near_rsem,
        device_id={"probe": 1 - core},
        device_id_type=MESH,
    )
    near_copy.start()

    own_coef.wait()

    def take_coef(k, carry):
        @pl.when(k != node)
        def _():
            coef_copy(k, k, node).wait_recv()

        return carry

    lax.fori_loop(0, nodes, take_coef, 0)
    ids = rows_ref[...]
    hits = (
        lax.broadcasted_iota(jnp.int32, (ids.shape[0], nodes * NODE_ROWS), 1) == ids
    ).astype(BF16)
    for rp in (0, 1):
        chosen = dot(hits, piece[rp])
        gathered[2 * rp] = chosen[:, :rank].astype(BF16)
        gathered[2 * rp + 1] = chosen[:, rank:].astype(BF16)

    lane = lax.broadcasted_iota(jnp.int32, (rank, 64), 1)
    fold = (
        lax.broadcasted_iota(jnp.int32, (8, 64), 1) // 16
        == lax.broadcasted_iota(jnp.int32, (8, 64), 0)
    ).astype(BF16)

    def couple(blocks, row, length):
        probes4 = jnp.concatenate(
            [gathered[r, pl.ds(row, 16), :] for r in range(4)], axis=0
        )
        full = dot(blocks, probes4, NT)
        total = jnp.zeros((rank, 64), F32)
        for m in range(length):
            total = total + jnp.where(
                lane % 16 == m, full[m * rank : (m + 1) * rank], 0.0
            )
        high = total.astype(BF16)
        low = (total - high.astype(F32)).astype(BF16)
        return dot(fold, high, NT) + dot(fold, low, NT)

    load0.wait()
    level_one = couple(
        coupling1_ref[0, 0].reshape(m1 * rank, rank), count * 16, m1
    ).astype(BF16)

    def far_leaf(i, carry):
        a, b = i // leaves_b, i % leaves_b
        total = couple(
            coupling0[a, b].reshape(m0 * rank, rank), pl.multiple_of(i * 16, 16), m0
        )
        total = (total + dot(level_one, transfer_ref[a, b])).astype(BF16)
        out_ref[a, b] = dot(total, basis_ref[a, b])[:4]
        return carry

    lax.fori_loop(0, count, far_leaf, 0)

    near_copy.wait()

    def add_near(i, carry):
        a, b = i // half, i % half
        for refs, at in ((near_mine, core), (near_theirs, 1 - core)):
            value = refs[i]
            value = jnp.where(core == 0, value[:4], value[4:])
            out_ref[a, at * half + b] += value
        return carry

    lax.fori_loop(0, leaves_a * half, add_near, 0)

    for ds, dt, to in halo_pieces():
        ok = exists(ds, dt)
        if ds == 0 and dt == 0:
            ok = core != to

        @pl.when(ok)
        def _(ds=ds, dt=dt, to=to):
            halo_copy(ds, dt, to, core, space + ds, tm + dt, to).wait_send()

    def end_coef(k, carry):
        @pl.when(k != node)
        def _():
            coef_copy(node, k, k).wait_send()

        return carry

    lax.fori_loop(0, nodes, end_coef, 0)


def on_device(
    n_space, n_tm, points, probes, basis, transfer, coupling0, list0, coupling1, list1, near
):
    leaves_a, leaves_b, _, width = points.shape
    rank = basis.shape[2]
    count = leaves_a * leaves_b
    half = leaves_b // 2
    columns = leaves_b * n_tm
    nodes = n_space * n_tm
    space = lax.axis_index("space")
    tm = lax.axis_index("tm")
    core = lax.axis_index("probe")

    pair_points = points.reshape(leaves_a, leaves_b // 2, 2, 3, width)
    chosen = jnp.where(core == 0, pair_points[:, :, 0], pair_points[:, :, 1])
    east = (space * leaves_a + jnp.arange(leaves_a)).astype(F32)[:, None] * CELL + CELL / 2
    hour = (tm * leaves_b + core + 2 * jnp.arange(leaves_b // 2)).astype(F32)[
        None, :
    ] * CELL + CELL / 2
    shape = (leaves_a, leaves_b // 2)
    middle = jnp.stack(
        [jnp.broadcast_to(east, shape), jnp.full(shape, CELL, F32), jnp.broadcast_to(hour, shape)],
        axis=2,
    )
    local = chosen - middle[..., None]
    high = lax.reduce_precision(local, 8, 7)
    low = local - high
    gap = jnp.zeros((leaves_a, leaves_b // 2, 1, width), BF16)
    pack = jnp.concatenate(
        [
            probes.reshape(leaves_a, leaves_b // 2, 8, width),
            high.astype(BF16),
            gap,
            low.astype(BF16),
            gap,
        ],
        axis=2,
    )

    mine = lax.dynamic_slice_in_dim(near, core * half, half, axis=1)
    slots = (mine // columns - (space * leaves_a - 2)) * (half + 4) + (
        mine % columns - (tm * leaves_b + core * half - 2)
    )
    slots = slots.reshape(-1)

    row, column = list0 // columns, list0 % columns
    leaf_rows = (
        (row // leaves_a * n_tm + column // leaves_b) * NODE_ROWS
        + row % leaves_a * leaves_b
        + column % leaves_b
    )
    leaf_rows = jnp.where(list0 < 0, -1, leaf_rows).reshape(count, -1)
    leaf_rows = jnp.pad(leaf_rows, ((0, 0), (0, 16 - leaf_rows.shape[1])), constant_values=-1)
    node_rows = jnp.where(list1 < 0, -1, list1 * NODE_ROWS + count).reshape(1, -1)
    node_rows = jnp.pad(node_rows, ((0, 0), (0, 16 - node_rows.shape[1])), constant_values=-1)
    rows = jnp.concatenate([leaf_rows, node_rows], axis=0).reshape(-1, 1)

    win_pairs = half // 2 + 2
    window = (leaves_a + 4) * win_pairs * 2
    vmem = pl.BlockSpec(memory_space=pltpu.VMEM)
    return pl.pallas_call(
        functools.partial(kernel, n_space, n_tm),
        out_shape=jax.ShapeDtypeStruct(probes.shape, F32),
        in_specs=[pl.BlockSpec(memory_space=pltpu.SMEM)]
        + [vmem] * 6
        + [pl.BlockSpec(memory_space=pl.ANY)],
        out_specs=vmem,
        scratch_shapes=[
            pltpu.VMEM((2, leaves_a + 4, win_pairs, 16, width), BF16),
            pltpu.VMEM((window, 32, width), BF16),
            pltpu.VMEM((leaves_a * win_pairs * 2, width, 32), BF16),
            pltpu.VMEM((window, 8, width), BF16),
            pltpu.VMEM((leaves_a * half, 8, width), F32),
            pltpu.VMEM((leaves_a * half, 8, width), F32),
            pltpu.VMEM((2, NODE_ROWS, 2 * rank), F32),
            pltpu.VMEM((2, NODE_ROWS, 2 * rank), BF16),
            pltpu.VMEM((2, nodes * NODE_ROWS, 2 * rank), BF16),
            pltpu.VMEM((4, (count + 1) * 16, rank), BF16),
            pltpu.VMEM(coupling0.shape, BF16),
            pltpu.SemaphoreType.DMA((3, 3, 2)),
            pltpu.SemaphoreType.DMA((2, 3, 3)),
            pltpu.SemaphoreType.DMA((nodes,)),
            pltpu.SemaphoreType.DMA((nodes,)),
            pltpu.SemaphoreType.DMA,
            pltpu.SemaphoreType.DMA,
            pltpu.SemaphoreType.DMA((3,)),
        ],
        compiler_params=pltpu.CompilerParams(
            collective_id=0, has_side_effects=True, vmem_limit_bytes=48 * 1024 * 1024
        ),
    )(slots, pack, probes, basis, transfer, coupling1, rows, coupling0)


def solution(mesh):
    in_specs = (
        P(("groups", "space"), "tm", None, None),
        P(("groups", "space"), "tm", "probe", None),
        P(("groups", "space"), "tm", None, None),
        P(("groups", "space"), "tm", None, None),
        P(("groups", "space"), "tm", None, None, None),
        P(("groups", "space"), "tm", None),
        P(("groups", "space"), "tm", None, None, None),
        P(("groups", "space"), "tm", None),
        P(("groups", "space"), "tm", None),
    )
    out_specs = P(("groups", "space"), "tm", "probe", None)
    return jax.shard_map(
        functools.partial(on_device, mesh.shape["space"], mesh.shape["tm"]),
        mesh=mesh,
        in_specs=in_specs,
        out_specs=out_specs,
        check_vma=False,
    )
```

time: 199 us -> 59.1 us (0.30)
  the two profiles are of different devices: /device:TPU:0 before, /device:TPU:1 now
where the time goes in v1:
time: 59.1 us; the launch traced here: 58.6 us
  Pallas kernels  48.8 us (83%)
  local copies, waits for them, and re-layouts  7.28 us (12%)
  other arithmetic  2.52 us (4%)
    pallas_call x1, Pallas kernels, on_device(): pl.pallas_call(functools.partial(kernel, n_space, n_tm), out_shape=jax.Sh...  48.8 us
    unnamed x10, local copies, waits for them, and re-layouts  5.62 us

profile of v1, /device:TPU:1, one launch (start us, length us, event | category | flops | bytes accessed | tf_op | source)
XLA Modules:
  0.0 58.6 jit_solution(16079667061673179824)
XLA Ops:
  0.0 0.7 %fusion.10 = s32[1,6]{1,0:T(1,128)S(1)} fusion(s32[1,1,6]{2,1,0:T(1,128)} %param.16), kind=kLoop, calls=%fused_computation.38 | loop fusion | flops 24 | bytes 48 | tf_op jit(solution)/shard_map/reshape | solution.py:416
  0.7 0.1 stack_broadcast_in_dim.4
  0.7 0.1 pad.13.clone
  0.8 0.1 pad_maximum_fusion
  0.9 0.1 copy.29
  1.0 0.8 %fusion.9 = s32[2,8,9]{1,0,2:T(2,128)S(1)} fusion(s32[2,16,9]{1,0,2:T(2,128)} %param.17, s32[]{:T(128)S(6)} %select_n.59, s32[]{:T(128)S(6)} %sub.53, s32[]{:T(128)S(6)} %sub.50), kind=kLoop, calls=%fused_computation.35 | loop fusion | flops 3312 | bytes 1164 | tf_op jit(solution)/shard_map/add | solution.py:403
  1.8 0.1 copy.25
  1.9 0.1 reshape.40.slots_ref
  2.0 0.9 %fusion.7 = s32[2,16,12]{1,0,2:T(2,128)S(1)} fusion(s32[2,16,12]{1,0,2:T(2,128)} %param.14), kind=kLoop, calls=%fused_computation.33 | loop fusion | flops 24576 | bytes 3072 | tf_op jit(solution)/shard_map/jit(_where)/select_n | solution.py:414
  2.8 0.1 copy.32
  2.9 0.9 %reshape.41 = bf16[2,8,8,256]{3,2,1,0:T(8,128)(2,1)S(1)} reshape(bf16[2,16,4,256]{3,2,1,0:T(4,128)(2,1)} %probes_ref.1) | data formatting | bytes 131072 | tf_op jit(solution)/shard_map/reshape | solution.py:393
  3.8 1.0 %copy.26 = f32[2,16,3,256]{3,0,2,1:T(2,128)S(1)} copy(f32[2,16,3,256]{3,1,2,0:T(8,128)} %param.9) | data formatting | bytes 196608 | tf_op args[0]
  4.8 0.1 fusion
  4.9 0.1 concatenate.6.pack_ref
  5.0 0.2 reshape.46.rows_ref
  5.2 0.0 copy-start
  5.2 1.2 %copy-done = bf16[2,16,64,256]{3,2,1,0:T(8,128)(2,1)S(1)} copy-done((bf16[2,16,64,256]{3,2,1,0:T(8,128)(2,1)S(1)}, bf16[2,16,64,256]{3,2,1,0:T(8,128)(2,1)}, u32[]{:S(2)}) %copy-start) | copy-done | bytes 1048600
  6.4 0.0 copy-start.1
  6.4 1.0 %copy-done.1 = bf16[2,16,64,64]{3,2,1,0:T(8,128)(2,1)S(1)} copy-done((bf16[2,16,64,64]{3,2,1,0:T(8,128)(2,1)S(1)}, bf16[2,16,64,64]{3,2,1,0:T(8,128)(2,1)}, u32[]{:S(2)}) %copy-start.1) | copy-done | bytes 262168
  7.5 0.0 copy-start.2
  7.5 0.8 %copy-done.2 = bf16[2,16,4,256]{3,2,1,0:T(4,128)(2,1)S(1)} copy-done((bf16[2,16,4,256]{3,2,1,0:T(4,128)(2,1)S(1)}, bf16[2,16,4,256]{3,2,1,0:T(4,128)(2,1)}, u32[]{:S(2)}) %copy-start.2) | copy-done | bytes 65560
  8.3 0.0 copy-start.3
  8.3 0.9 %copy-done.3 = bf16[1,1,6,64,64]{4,3,2,1,0:T(8,128)(2,1)S(1)} copy-done((bf16[1,1,6,64,64]{4,3,2,1,0:T(8,128)(2,1)S(1)}, bf16[1,1,6,64,64]{4,3,2,1,0:T(8,128)(2,1)}, u32[]{:S(2)}) %copy-start.3) | copy-done | bytes 49176
  9.2 48.8 %shard_map.91 = f32[2,16,4,256]{3,2,1,0:T(4,128)S(1)} custom-call(s32[144]{0:T(256)S(1)} %reshape.40.slots_ref, bf16[2,8,16,256]{3,2,1,0:T(8,128)(2,1)S(1)} %concatenate.6.pack_ref, bf16[2,16,4,256]{3,2,1,0:T(4,128)(2,1)S(1)} %copy-done.2, bf16[2,16,64,256]{3,2,1,0:T(8,128)(2,1)S(1)} %copy-done, bf16[2,16,64,64]{3,2,1,0:T(8,128)(2,1)S(1)} %copy-done.1, ...), custom_call_target="tpu_custom_call" | custom-call | tf_op jit(solution)/shard_map/pallas_call | solution.py:423
  58.0 0.7 %copy.50 = f32[2,16,4,256]{3,2,1,0:T(4,128)} copy(f32[2,16,4,256]{3,2,1,0:T(4,128)S(1)} %shard_map.91) | data formatting | bytes 262144
  (6 shorter events, 0.0 us)
Async XLA Ops:
  5.2 1.2 %copy-start = (bf16[2,16,64,256]{3,2,1,0:T(8,128)(2,1)S(1)}, bf16[2,16,64,256]{3,2,1,0:T(8,128)(2,1)}, u32[]{:S(2)}) copy-start(bf16[2,16,64,256]{3,2,1,0:T(8,128)(2,1)} %basis_ref.1) | copy-start | bytes 3145732
  6.4 1.0 %copy-start.1 = (bf16[2,16,64,64]{3,2,1,0:T(8,128)(2,1)S(1)}, bf16[2,16,64,64]{3,2,1,0:T(8,128)(2,1)}, u32[]{:S(2)}) copy-start(bf16[2,16,64,64]{3,2,1,0:T(8,128)(2,1)} %transfer_ref.1) | copy-start | bytes 786436
  7.5 0.8 %copy-start.2 = (bf16[2,16,4,256]{3,2,1,0:T(4,128)(2,1)S(1)}, bf16[2,16,4,256]{3,2,1,0:T(4,128)(2,1)}, u32[]{:S(2)}) copy-start(bf16[2,16,4,256]{3,2,1,0:T(4,128)(2,1)} %probes_ref.1) | copy-start | bytes 196612
  8.3 0.9 %copy-start.3 = (bf16[1,1,6,64,64]{4,3,2,1,0:T(8,128)(2,1)S(1)}, bf16[1,1,6,64,64]{4,3,2,1,0:T(8,128)(2,1)}, u32[]{:S(2)}) copy-start(bf16[1,1,6,64,64]{4,3,2,1,0:T(8,128)(2,1)} %coupling1_ref.1) | copy-start | bytes 147460

commit v2 on v1

--- a/solution.py
+++ b/solution.py
@@ -15,6 +15,7 @@
 LOG2E = math.log2(math.e)
 SPACE_SCALE = math.sqrt(LOG2E / (4.5 * CELL * CELL))
 TIME_SCALE = math.sqrt(LOG2E / (2.0 * CELL * CELL))
+GROUP = 4
 NODE_ROWS = 48
 
 NT = (((1,), (1,)), ((), ()))
@@ -34,15 +35,28 @@
 def kernel(
     n_space,
     n_tm,
-    slots_ref,
-    pack_ref,
+    points_hbm,
+    probes_hbm,
+    basis_hbm,
+    transfer_hbm,
+    coupling0_hbm,
+    list0_hbm,
+    coupling1_hbm,
+    list1_hbm,
+    near_hbm,
+    out_ref,
+    points_ref,
     probes_ref,
     basis_ref,
     transfer_ref,
+    coupling0,
+    list0_ref,
     coupling1_ref,
-    rows_ref,
-    coupling0_hbm,
-    out_ref,
+    list1_ref,
+    near_ref,
+    pack_ref,
+    ids_ref,
+    hits_ref,
     win,
     other_feat,
     own_feat,
@@ -53,7 +67,6 @@
     coef_send,
     piece,
     gathered,
-    coupling0,
     halo_send,
     halo_recv,
     coef_ssem,
@@ -77,8 +90,23 @@
     m1 = coupling1_ref.shape[2]
     rank = basis_ref.shape[2]
 
-    load0 = pltpu.make_async_copy(coupling0_hbm, coupling0, local_sem.at[0])
-    load0.start()
+    columns = leaves_b * n_tm
+    loads = {}
+    for at, (name, source, target) in enumerate(
+        (
+            ("points", points_hbm, points_ref),
+            ("probes", probes_hbm, probes_ref),
+            ("basis", basis_hbm, basis_ref),
+            ("transfer", transfer_hbm, transfer_ref),
+            ("list0", list0_hbm, list0_ref),
+            ("list1", list1_hbm, list1_ref),
+            ("near", near_hbm, near_ref),
+            ("coupling1", coupling1_hbm, coupling1_ref),
+            ("coupling0", coupling0_hbm, coupling0),
+        )
+    ):
+        loads[name] = pltpu.make_async_copy(source, target, local_sem.at[at + 3])
+        loads[name].start()
 
     barrier = pltpu.get_barrier_semaphore()
 
@@ -99,6 +127,30 @@
         return carry
 
     lax.fori_loop(0, 2 * nodes, greet, 0)
+
+    loads["points"].wait()
+    loads["probes"].wait()
+    row3 = lax.broadcasted_iota(jnp.int32, (3, 1), 0)
+    zero1 = jnp.zeros((1, 256), F32)
+    for a in range(leaves_a):
+        for j in range(pairs):
+            east = ((space * leaves_a + a) * CELL + CELL // 2).astype(F32)
+            hour = ((tm * leaves_b + 2 * j + core) * CELL + CELL // 2).astype(F32)
+            middle = jnp.where(row3 == 0, east, jnp.where(row3 == 2, hour, float(CELL)))
+            at = points_ref[a, 2 * j + core] - middle
+            high = at.astype(BF16).astype(F32)
+            tile = jnp.concatenate(
+                [
+                    probes_ref[a, 2 * j].astype(F32),
+                    probes_ref[a, 2 * j + 1].astype(F32),
+                    high,
+                    zero1,
+                    at - high,
+                    zero1,
+                ],
+                axis=0,
+            )
+            pack_ref[a, j] = tile.astype(BF16)
     pl.semaphore_wait(barrier, 2 * nodes - 1)
 
     def halo_pieces():
@@ -147,6 +199,8 @@
         def _(ds=ds, dt=dt, to=to):
             halo_copy(ds, dt, to, core, space + ds, tm + dt, to).start()
 
+    loads["basis"].wait()
+    loads["transfer"].wait()
     node_sum = jnp.zeros((4, rank), F32)
     for i in range(count):
         a, b = i // leaves_b, i % leaves_b
@@ -188,6 +242,30 @@
     )
     own_coef.start()
 
+    loads["list0"].wait()
+    loads["list1"].wait()
+    ids_ref[...] = jnp.full(ids_ref.shape, -1.0, F32)
+    for a in range(leaves_a):
+        named = list0_ref[a]
+        row, column = named // columns, named % columns
+        place = (
+            (row // leaves_a * n_tm + column // leaves_b) * NODE_ROWS
+            + row % leaves_a * leaves_b
+            + column % leaves_b
+        )
+        ids_ref[a, :, pl.ds(0, m0)] = jnp.where(named < 0, -1, place).astype(F32)
+    named = list1_ref[0]
+    ids_ref[leaves_a, pl.ds(0, 1), pl.ds(0, m1)] = jnp.where(
+        named < 0, -1, named * NODE_ROWS + count
+    ).astype(F32)
+    spread = lax.broadcasted_iota(jnp.int32, (16, nodes * NODE_ROWS), 1).astype(F32)
+    for a in range(leaves_a + 1):
+        turned = ids_ref[a].T
+        for b in range(leaves_b if a < leaves_a else 1):
+            hits_ref[pl.ds((a * leaves_b + b) * 16, 16)] = jnp.where(
+                turned[:16, b : b + 1] == spread, 1.0, 0.0
+            ).astype(BF16)
+
     own_copy.wait()
     for source in (0, 1):
         for ds in (-1, 0, 1):
@@ -216,11 +294,15 @@
     row4 = lax.broadcasted_iota(jnp.int32, (4, 1), 0)
     scale = jnp.where(row4 == 2, TIME_SCALE, jnp.where(row4 == 3, 0.0, SPACE_SCALE))
     ones = jnp.where(lax.broadcasted_iota(jnp.int32, (4, 256), 0) < 3, 1.0, 0.0).astype(F32)
-    zero1 = jnp.zeros((1, 256), F32)
     mid_a = (leaves_a + 4) / 2.0 - 0.5
     mid_b = (half + 4) / 2.0 - 0.5
 
-    def features(w, j, carry):
+    def features(w, step, carry):
+        for part in range(3):
+            pair_features(w, step * 3 + part)
+        return carry
+
+    def pair_features(w, j):
         tiles = [win[s, w, j].astype(F32) for s in (0, 1)]
         for e in (0, 1):
             slot = (w * win_pairs + j) * 2 + e
@@ -245,18 +327,22 @@
                 high, mid, low = 2.0 * high, 2.0 * mid, 2.0 * low
                 feat = jnp.concatenate([high, high, high, mid, mid, low, ones, norms], axis=0)
                 own_feat[(w - 2) * win_pairs * 2 + j * 2 + e] = feat.T.astype(BF16)
-        return carry
 
     for w in range(leaves_a + 4):
-        lax.fori_loop(0, win_pairs, functools.partial(features, w), 0)
-
-    picks = slots_ref.shape[0] // (leaves_a * half)
+        lax.fori_loop(0, win_pairs // 3, functools.partial(features, w), 0)
+
+    loads["near"].wait()
+    picks = near_hbm.shape[2]
+    first_a = space * leaves_a - 2
+    first_b = tm * leaves_b + core * half - 2
 
     def near_leaf(i, carry):
         own = own_feat[i // half * (2 * win_pairs) + i % half + 2]
         total = jnp.zeros((own.shape[0], 8), F32)
         for n in range(picks):
-            slot = slots_ref[i * picks + n]
+            named = near_ref[i // half, core * half + i % half, n]
+            slot = (named // columns - first_a) * (half + 4) + named % columns - first_b
+            slot = jnp.clip(slot, 0, other_feat.shape[0] - 1)
             kern = jnp.exp2(dot(own, other_feat[slot])).astype(BF16)
             total = total + dot(kern, vectors[slot], NT)
         near_mine[i] = total.T
@@ -284,10 +370,7 @@
         return carry
 
     lax.fori_loop(0, nodes, take_coef, 0)
-    ids = rows_ref[...]
-    hits = (
-        lax.broadcasted_iota(jnp.int32, (ids.shape[0], nodes * NODE_ROWS), 1) == ids
-    ).astype(BF16)
+    hits = hits_ref[...]
     for rp in (0, 1):
         chosen = dot(hits, piece[rp])
         gathered[2 * rp] = chosen[:, :rank].astype(BF16)
@@ -313,33 +396,41 @@
         low = (total - high.astype(F32)).astype(BF16)
         return dot(fold, high, NT) + dot(fold, low, NT)
 
-    load0.wait()
+    loads["coupling1"].wait()
+    loads["coupling0"].wait()
     level_one = couple(
         coupling1_ref[0, 0].reshape(m1 * rank, rank), count * 16, m1
     ).astype(BF16)
 
-    def far_leaf(i, carry):
-        a, b = i // leaves_b, i % leaves_b
-        total = couple(
-            coupling0[a, b].reshape(m0 * rank, rank), pl.multiple_of(i * 16, 16), m0
-        )
-        total = (total + dot(level_one, transfer_ref[a, b])).astype(BF16)
-        out_ref[a, b] = dot(total, basis_ref[a, b])[:4]
-        return carry
-
-    lax.fori_loop(0, count, far_leaf, 0)
+    def far_leaves(step, carry):
+        a, b = step // (leaves_b // GROUP), step % (leaves_b // GROUP) * GROUP
+        totals = [
+            couple(
+                coupling0[a, b + g].reshape(m0 * rank, rank),
+                pl.multiple_of((step * GROUP + g) * 16, 16),
+                m0,
+            )
+            for g in range(GROUP)
+        ]
+        totals = [
+            (totals[g] + dot(level_one, transfer_ref[a, b + g])).astype(BF16)
+            for g in range(GROUP)
+        ]
+        values = [dot(totals[g], basis_ref[a, b + g])[:4] for g in range(GROUP)]
+        for g in range(GROUP):
+            out_ref[a, b + g] = values[g]
+        return carry
+
+    lax.fori_loop(0, count // GROUP, far_leaves, 0)
 
     near_copy.wait()
 
-    def add_near(i, carry):
+    for i in range(leaves_a * half):
         a, b = i // half, i % half
         for refs, at in ((near_mine, core), (near_theirs, 1 - core)):
             value = refs[i]
             value = jnp.where(core == 0, value[:4], value[4:])
             out_ref[a, at * half + b] += value
-        return carry
-
-    lax.fori_loop(0, leaves_a * half, add_near, 0)
 
     for ds, dt, to in halo_pieces():
         ok = exists(ds, dt)
@@ -367,67 +458,22 @@
     rank = basis.shape[2]
     count = leaves_a * leaves_b
     half = leaves_b // 2
-    columns = leaves_b * n_tm
     nodes = n_space * n_tm
-    space = lax.axis_index("space")
-    tm = lax.axis_index("tm")
-    core = lax.axis_index("probe")
-
-    pair_points = points.reshape(leaves_a, leaves_b // 2, 2, 3, width)
-    chosen = jnp.where(core == 0, pair_points[:, :, 0], pair_points[:, :, 1])
-    east = (space * leaves_a + jnp.arange(leaves_a)).astype(F32)[:, None] * CELL + CELL / 2
-    hour = (tm * leaves_b + core + 2 * jnp.arange(leaves_b // 2)).astype(F32)[
-        None, :
-    ] * CELL + CELL / 2
-    shape = (leaves_a, leaves_b // 2)
-    middle = jnp.stack(
-        [jnp.broadcast_to(east, shape), jnp.full(shape, CELL, F32), jnp.broadcast_to(hour, shape)],
-        axis=2,
-    )
-    local = chosen - middle[..., None]
-    high = lax.reduce_precision(local, 8, 7)
-    low = local - high
-    gap = jnp.zeros((leaves_a, leaves_b // 2, 1, width), BF16)
-    pack = jnp.concatenate(
-        [
-            probes.reshape(leaves_a, leaves_b // 2, 8, width),
-            high.astype(BF16),
-            gap,
-            low.astype(BF16),
-            gap,
-        ],
-        axis=2,
-    )
-
-    mine = lax.dynamic_slice_in_dim(near, core * half, half, axis=1)
-    slots = (mine // columns - (space * leaves_a - 2)) * (half + 4) + (
-        mine % columns - (tm * leaves_b + core * half - 2)
-    )
-    slots = slots.reshape(-1)
-
-    row, column = list0 // columns, list0 % columns
-    leaf_rows = (
-        (row // leaves_a * n_tm + column // leaves_b) * NODE_ROWS
-        + row % leaves_a * leaves_b
-        + column % leaves_b
-    )
-    leaf_rows = jnp.where(list0 < 0, -1, leaf_rows).reshape(count, -1)
-    leaf_rows = jnp.pad(leaf_rows, ((0, 0), (0, 16 - leaf_rows.shape[1])), constant_values=-1)
-    node_rows = jnp.where(list1 < 0, -1, list1 * NODE_ROWS + count).reshape(1, -1)
-    node_rows = jnp.pad(node_rows, ((0, 0), (0, 16 - node_rows.shape[1])), constant_values=-1)
-    rows = jnp.concatenate([leaf_rows, node_rows], axis=0).reshape(-1, 1)
-
+    args = (points, probes, basis, transfer, coupling0, list0, coupling1, list1, near)
     win_pairs = half // 2 + 2
     window = (leaves_a + 4) * win_pairs * 2
     vmem = pl.BlockSpec(memory_space=pltpu.VMEM)
     return pl.pallas_call(
         functools.partial(kernel, n_space, n_tm),
         out_shape=jax.ShapeDtypeStruct(probes.shape, F32),
-        in_specs=[pl.BlockSpec(memory_space=pltpu.SMEM)]
-        + [vmem] * 6
-        + [pl.BlockSpec(memory_space=pl.ANY)],
+        in_specs=[pl.BlockSpec(memory_space=pl.ANY)] * len(args),
         out_specs=vmem,
-        scratch_shapes=[
+        scratch_shapes=[pltpu.VMEM(value.shape, value.dtype) for value in args[:-1]]
+        + [
+            pltpu.SMEM(near.shape, near.dtype),
+            pltpu.VMEM((leaves_a, leaves_b // 2, 16, width), BF16),
+            pltpu.VMEM((leaves_a + 1, leaves_b, 128), F32),
+            pltpu.VMEM(((count + 1) * 16, nodes * NODE_ROWS), BF16),
             pltpu.VMEM((2, leaves_a + 4, win_pairs, 16, width), BF16),
             pltpu.VMEM((window, 32, width), BF16),
             pltpu.VMEM((leaves_a * win_pairs * 2, width, 32), BF16),
@@ -438,19 +484,18 @@
             pltpu.VMEM((2, NODE_ROWS, 2 * rank), BF16),
             pltpu.VMEM((2, nodes * NODE_ROWS, 2 * rank), BF16),
             pltpu.VMEM((4, (count + 1) * 16, rank), BF16),
-            pltpu.VMEM(coupling0.shape, BF16),
             pltpu.SemaphoreType.DMA((3, 3, 2)),
             pltpu.SemaphoreType.DMA((2, 3, 3)),
             pltpu.SemaphoreType.DMA((nodes,)),
             pltpu.SemaphoreType.DMA((nodes,)),
             pltpu.SemaphoreType.DMA,
             pltpu.SemaphoreType.DMA,
-            pltpu.SemaphoreType.DMA((3,)),
+            pltpu.SemaphoreType.DMA((12,)),
         ],
         compiler_params=pltpu.CompilerParams(
-            collective_id=0, has_side_effects=True, vmem_limit_bytes=48 * 1024 * 1024
+            collective_id=0, has_side_effects=True, vmem_limit_bytes=60 * 1024 * 1024
         ),
-    )(slots, pack, probes, basis, transfer, coupling1, rows, coupling0)
+    )(*args)
 
 
 def solution(mesh):

time: 59.1 us -> 48.5 us (0.82)
  Pallas kernels: 48.8 us -> 42.3 us
  other arithmetic: 2.52 us -> 0 us
  local copies, waits for them, and re-layouts: 7.28 us -> 5.94 us
    pallas_call x1, Pallas kernels: 48.8 us -> 42.3 us  [on_device(): pl.pallas_call(functools.partial(kernel, n_space, n_tm), out_shape=jax.Sh...]
    reshape x4 -> x0, local copies, waits for them, and re-layouts: 1.22 us -> none  [the longest x1 0.86 us: on_device(): probes.reshape(leaves_a, leaves_b // 2, 8, width)]
    select_n x1 -> x0, other arithmetic: 0.85 us -> none  [on_device(): leaf_rows = jnp.where(list0 < 0, -1, leaf_rows).reshape(count, -1)]
    add x3 -> x0, other arithmetic: 0.82 us -> none  [the longest x1 0.81 us: on_device(): (mine // columns - (space * leaves_a - 2)) * (half + 4)]
    reshape x1 -> x0, other arithmetic: 0.66 us -> none  [on_device(): jnp.where(list1 < 0, -1, list1 * NODE_ROWS + count).reshape(1, -1)]
    unnamed x10 -> x4, local copies, waits for them, and re-layouts: 5.62 us -> 5.94 us
where the time goes in v2:
time: 48.5 us; the launch traced here: 48.2 us
  Pallas kernels  42.3 us (87%)
  local copies, waits for them, and re-layouts  5.94 us (12%)
    pallas_call x1, Pallas kernels, on_device(): pl.pallas_call(functools.partial(kernel, n_space, n_tm), out_shape=jax.Sh...  42.3 us
    unnamed x4, local copies, waits for them, and re-layouts  5.94 us

profile of v2, /device:TPU:1, one launch (start us, length us, event | category | flops | bytes accessed | tf_op | source)
XLA Modules:
  0.0 48.2 jit_solution(8301907488594089724)
XLA Ops:
  0.0 1.4 %copy.11.list0_hbm = s32[2,16,12]{2,1,0:T(8,128)} copy(s32[2,16,12]{1,0,2:T(2,128)} %param.14) | data formatting | bytes 3072 | tf_op args[5]
  1.4 1.4 %copy.12.near_hbm = s32[2,16,9]{2,1,0:T(8,128)} copy(s32[2,16,9]{1,0,2:T(2,128)} %param.17) | data formatting | bytes 2304 | tf_op args[8]
  2.8 1.6 %copy.10.points_hbm = f32[2,16,3,256]{3,2,1,0:T(4,128)} copy(f32[2,16,3,256]{3,1,2,0:T(8,128)} %param.9) | data formatting | bytes 196608 | tf_op args[0]
  4.4 42.3 %shard_map.91 = f32[2,16,4,256]{3,2,1,0:T(4,128)} custom-call(f32[2,16,3,256]{3,2,1,0:T(4,128)} %copy.10.points_hbm, bf16[2,16,4,256]{3,2,1,0:T(4,128)(2,1)} %probes_hbm.1, bf16[2,16,64,256]{3,2,1,0:T(8,128)(2,1)} %basis_hbm.1, bf16[2,16,64,64]{3,2,1,0:T(8,128)(2,1)} %transfer_hbm.1, bf16[2,16,12,64,64]{4,3,2,1,0:T(8,128)(2,1)} %coupling0_hbm.1, ...), custom_call_target="tpu_custom_call" | custom-call | tf_op jit(solution)/shard_map/pallas_call | solution.py:466
  46.7 1.6 %copy.14 = f32[2,16,4,256]{3,2,1,0:T(4,128)} copy(f32[2,16,4,256]{3,2,1,0:T(4,128)} %shard_map.91) | data formatting | bytes 262144

commit v3 on v2

--- a/solution.py
+++ b/solution.py
@@ -15,7 +15,7 @@
 LOG2E = math.log2(math.e)
 SPACE_SCALE = math.sqrt(LOG2E / (4.5 * CELL * CELL))
 TIME_SCALE = math.sqrt(LOG2E / (2.0 * CELL * CELL))
-GROUP = 4
+GROUP = 8
 NODE_ROWS = 48
 
 NT = (((1,), (1,)), ((), ()))
@@ -338,14 +338,14 @@
 
     def near_leaf(i, carry):
         own = own_feat[i // half * (2 * win_pairs) + i % half + 2]
-        total = jnp.zeros((own.shape[0], 8), F32)
+        total = jnp.zeros((8, own.shape[0]), F32)
         for n in range(picks):
             named = near_ref[i // half, core * half + i % half, n]
             slot = (named // columns - first_a) * (half + 4) + named % columns - first_b
             slot = jnp.clip(slot, 0, other_feat.shape[0] - 1)
             kern = jnp.exp2(dot(own, other_feat[slot])).astype(BF16)
-            total = total + dot(kern, vectors[slot], NT)
-        near_mine[i] = total.T
+            total = total + dot(vectors[slot], kern, NT)
+        near_mine[i] = total
         return carry
 
     lax.fori_loop(0, leaves_a * half, near_leaf, 0)

time: 48.5 us -> 47.1 us (0.971)
  Pallas kernels: 42.3 us -> 40.8 us
    pallas_call x1, Pallas kernels: 42.3 us -> 40.8 us  [on_device(): pl.pallas_call(functools.partial(kernel, n_space, n_tm), out_shape=jax.Sh...]
where the time goes in v3:
time: 47.1 us; the launch traced here: 46.8 us
  Pallas kernels  40.8 us (87%)
  local copies, waits for them, and re-layouts  5.94 us (13%)
    pallas_call x1, Pallas kernels, on_device(): pl.pallas_call(functools.partial(kernel, n_space, n_tm), out_shape=jax.Sh...  40.8 us
    unnamed x4, local copies, waits for them, and re-layouts  5.94 us

profile of v3, /device:TPU:1, one launch (start us, length us, event | category | flops | bytes accessed | tf_op | source)
XLA Modules:
  0.0 46.8 jit_solution(15221923751082919878)
XLA Ops:
  0.0 1.4 %copy.11.list0_hbm = s32[2,16,12]{2,1,0:T(8,128)} copy(s32[2,16,12]{1,0,2:T(2,128)} %param.14) | data formatting | bytes 3072 | tf_op args[5]
  1.4 1.4 %copy.12.near_hbm = s32[2,16,9]{2,1,0:T(8,128)} copy(s32[2,16,9]{1,0,2:T(2,128)} %param.17) | data formatting | bytes 2304 | tf_op args[8]
  2.8 1.6 %copy.10.points_hbm = f32[2,16,3,256]{3,2,1,0:T(4,128)} copy(f32[2,16,3,256]{3,1,2,0:T(8,128)} %param.9) | data formatting | bytes 196608 | tf_op args[0]
  4.4 40.8 %shard_map.91 = f32[2,16,4,256]{3,2,1,0:T(4,128)} custom-call(f32[2,16,3,256]{3,2,1,0:T(4,128)} %copy.10.points_hbm, bf16[2,16,4,256]{3,2,1,0:T(4,128)(2,1)} %probes_hbm.1, bf16[2,16,64,256]{3,2,1,0:T(8,128)(2,1)} %basis_hbm.1, bf16[2,16,64,64]{3,2,1,0:T(8,128)(2,1)} %transfer_hbm.1, bf16[2,16,12,64,64]{4,3,2,1,0:T(8,128)(2,1)} %coupling0_hbm.1, ...), custom_call_target="tpu_custom_call" | custom-call | tf_op jit(solution)/shard_map/pallas_call | solution.py:466
  45.2 1.6 %copy.14 = f32[2,16,4,256]{3,2,1,0:T(4,128)} copy(f32[2,16,4,256]{3,2,1,0:T(4,128)} %shard_map.91) | data formatting | bytes 262144
